TPU v7x, 256 devices: a whole 4x4x8 slice. The times are simulated.
256 devices in a mesh: dp: 32 (over y_hi, z, core), proto: 8 (over y_lo, x).
Axes of the slice: x: 4, y: 4 (y_hi: 2, y_lo: 2; y = y_hi * 2 + y_lo), z: 8, core: 2. Of those that a mesh axis runs over, the one named last changes fastest.
Arguments:
- cls_features: bfloat16 [128, 384], P('dp')
- patch_features: bfloat16 [128, 256, 384], P('dp')
- mask_index: int32 [128, 64], P('dp'), may hold values from 0 to 255, as said below
- cls_protos: bfloat16 [384, 131072], P(None, ('proto', 'dp'))
- patch_protos: bfloat16 [384, 131072], P(None, ('proto', 'dp'))
Outputs:
- cls_targets: bfloat16 [128, 131072], P('dp', 'proto')
- patch_targets: bfloat16 [8192, 131072], P('dp', 'proto')
Inputs may be any that keep to these rules, and one draw needn't show every extreme that they name: `mask_index`: the 64 numbers of one crop are distinct.
All inputs are finite; a program needn't handle non-finite values.
Results may differ from a plain program's by a relative error of at most 0.0036.
Values may be sent and summed in bfloat16 or wider, within the bound.
No kernel may reach another device: no remote copies, remote signals or barrier semaphores. Data moves between devices by JAX's collectives and lax.ppermute only.
A program may use at most 128 MiB of HBM per device.

v0:
```python
import jax
import jax.numpy as jnp
from jax import lax
from jax.sharding import PartitionSpec as P

PROTOS = 131072
ITERS = 3


teacher_temp = 0.07


def unit_rows(values):
    wide = values.astype(jnp.float32)
    return (wide * lax.rsqrt(jnp.sum(wide * wide, -1, keepdims=True) + 1e-06)).astype(jnp.bfloat16)


def kernel_of(units, protos):
    wide = protos.astype(jnp.float32)
    colsq = jnp.sum(wide * wide, 0)
    cosine = jnp.dot(units, protos, preferred_element_type=jnp.float32) * lax.rsqrt(colsq + 1e-06)
    return jnp.exp((cosine - 1.0) / teacher_temp)


def column_terms(row_scale, kernel):
    return jnp.dot(row_scale, kernel, precision=lax.Precision.HIGHEST)


def row_terms(kernel, col_scale):
    return jnp.dot(kernel, col_scale, precision=lax.Precision.HIGHEST)


def scaled(kernel, row_scale, col_scale):
    return (PROTOS * row_scale[:, None] * kernel * col_scale[None, :]).astype(jnp.bfloat16)


def per_device(cls_features, patch_features, mask_index, cls_protos, patch_protos):
    selected = jnp.take_along_axis(patch_features, mask_index[:, :, None], axis=1)
    patch_unit = unit_rows(selected.reshape(-1, selected.shape[2]))
    cls_unit = unit_rows(cls_features)
    patch_kernel = kernel_of(patch_unit, lax.all_gather(patch_protos, "dp", axis=1, tiled=True))
    cls_kernel = kernel_of(cls_unit, lax.all_gather(cls_protos, "dp", axis=1, tiled=True))
    patch_row_scale = jnp.ones((patch_kernel.shape[0],), jnp.float32)
    cls_row_scale = jnp.ones((cls_kernel.shape[0],), jnp.float32)
    for step in range(ITERS):
        column_sums = lax.psum(
            (column_terms(patch_row_scale, patch_kernel), column_terms(cls_row_scale, cls_kernel)),
            "dp",
        )
        patch_col_scale = 1.0 / column_sums[0]
        cls_col_scale = 1.0 / column_sums[1]
        row_sums = lax.psum(
            (row_terms(patch_kernel, patch_col_scale), row_terms(cls_kernel, cls_col_scale)),
            "proto",
        )
        patch_row_scale = 1.0 / row_sums[0]
        cls_row_scale = 1.0 / row_sums[1]
    patch_targets = scaled(patch_kernel, patch_row_scale, patch_col_scale)
    cls_targets = scaled(cls_kernel, cls_row_scale, cls_col_scale)
    return (cls_targets, patch_targets)


def solution(mesh):
    return jax.shard_map(
        per_device,
        mesh=mesh,
        in_specs=(
            P("dp", None),
            P("dp", None, None),
            P("dp", None),
            P(None, ("proto", "dp")),
            P(None, ("proto", "dp")),
        ),
        out_specs=(P("dp", "proto"), P("dp", "proto")),
        check_vma=False,
    )
```

profile of v0, /device:TPU:1, one launch (start us, length us, event | category | flops | bytes accessed | tf_op | source)
XLA Modules:
  0.0 1154.2 jit_solution(4762158097622119005)
XLA Ops:
  10.3 1.9 gather_fusion
  12.5 0.8 fusion.10
  13.3 131.4 %all-gather.5.cloned.1.call-done = bf16[384,16384]{1,0:T(8,128)(2,1)} async-done(((bf16[384,512]{1,0:T(8,128)(2,1)}), bf16[384,16384]{1,0:T(8,128)(2,1)}) %all-gather.5.cloned.1.call-update) | async-done | bytes 12582928 | tf_op jit(solution)/shard_map/all_gather | solution.py:41
  144.7 7.3 multiply_reduce_fusion
  152.0 8.6 fusion.2
  160.6 5.7 copy-done.1
  166.3 8.6 fusion.14
  174.9 98.5 %all-gather.3.cloned.1.call-done = bf16[384,16384]{1,0:T(8,128)(2,1)} async-done(((bf16[384,512]{1,0:T(8,128)(2,1)}), bf16[384,16384]{1,0:T(8,128)(2,1)}) %all-gather.3.cloned.1.call-update) | async-done | bytes 12582928 | tf_op jit(solution)/shard_map/all_gather | solution.py:42
  273.4 7.3 multiply_reduce_fusion.1
  280.8 6.5 fusion.5
  287.3 1.2 fusion.22
  288.5 239.0 %all-reduce.14.cloned.1.call-done = (f32[16384]{0:T(1024)}, f32[16384]{0:T(1024)}) async-done(((f32[16384]{0:T(1024)}, f32[16384]{0:T(1024)}), (f32[16384]{0:T(1024)}, f32[16384]{0:T(1024)})) %all-reduce.14.cloned.1.call-update) | async-done | bytes 131088 | tf_op jit(solution)/shard_map/psum | solution.py:46
  527.6 0.9 broadcast_divide_fusion.2
  528.5 16.1 %fusion.31 = f32[1,256]{1,0:T(1,128)S(1)} fusion(f32[256,16384]{1,0:T(8,128)} %copy-done.1, f32[16384,1]{0,1:T(1,128)S(1)} %bitcast.62), kind=kOutput, calls=%fused_computation.61 | convolution fusion | flops 50331648 | bytes 16843776 | tf_op jit(solution)/shard_map/dot_general | solution.py:30
  544.5 1.3 convolution_bitcast_fusion.2
  545.8 14.9 %all-reduce.5 = (f32[4]{0:T(128)S(1)}, f32[256]{0:T(256)S(1)}) all-reduce(f32[4]{0:T(128)S(1)} %convolution_bitcast_fusion.2, f32[256]{0:T(256)S(1)} %bitcast.72), channel_id=1, replica_groups=mesh['dp'=32,'proto'=8] {'proto'}, use_global_device_ids=true, to_apply=%region_3.4 | all-reduce | flops 260 | bytes 2080 | tf_op jit(solution)/shard_map/psum | solution.py:52
  560.7 12.1 %fusion.32 = f32[1,16384]{1,0:T(1,128)} fusion(f32[256,1]{0,1:T(1,128)S(1)} %bitcast.69, f32[256,16384]{1,0:T(8,128)} %copy-done.1), kind=kOutput, calls=%fused_computation.62 | convolution fusion | flops 50331648 | bytes 16843776 | tf_op jit(solution)/shard_map/dot_general | solution.py:26
  572.8 1.2 fusion.18
  574.0 241.6 %all-reduce.12.cloned.1.call-done = (f32[16384]{0:T(1024)}, f32[16384]{0:T(1024)}) async-done(((f32[16384]{0:T(1024)}, f32[16384]{0:T(1024)}), (f32[16384]{0:T(1024)}, f32[16384]{0:T(1024)})) %all-reduce.12.cloned.1.call-update) | async-done | bytes 131088 | tf_op jit(solution)/shard_map/psum | solution.py:46
  815.7 0.9 broadcast_divide_fusion.1
  816.6 16.3 %fusion.33 = f32[1,256]{1,0:T(1,128)S(1)} fusion(f32[256,16384]{1,0:T(8,128)} %copy-done.1, f32[16384,1]{0,1:T(1,128)S(1)} %bitcast.61), kind=kOutput, calls=%fused_computation.63 | convolution fusion | flops 50331648 | bytes 16843776 | tf_op jit(solution)/shard_map/dot_general | solution.py:30
  832.9 1.2 convolution_bitcast_fusion.1
  834.1 14.9 %all-reduce.4 = (f32[4]{0:T(128)S(1)}, f32[256]{0:T(256)S(1)}) all-reduce(f32[4]{0:T(128)S(1)} %convolution_bitcast_fusion.1, f32[256]{0:T(256)S(1)} %bitcast.71), channel_id=1, replica_groups=mesh['dp'=32,'proto'=8] {'proto'}, use_global_device_ids=true, to_apply=%region_5.6 | all-reduce | flops 260 | bytes 2080 | tf_op jit(solution)/shard_map/psum | solution.py:52
  849.0 12.1 %fusion.34 = f32[1,16384]{1,0:T(1,128)} fusion(f32[256,1]{0,1:T(1,128)S(1)} %bitcast.70, f32[256,16384]{1,0:T(8,128)} %copy-done.1), kind=kOutput, calls=%fused_computation.64 | convolution fusion | flops 50331648 | bytes 16843776 | tf_op jit(solution)/shard_map/dot_general | solution.py:26
  861.1 1.2 fusion.16
  862.3 241.7 %all-reduce.10.cloned.1.call-done = (f32[16384]{0:T(1024)}, f32[16384]{0:T(1024)}) async-done(((f32[16384]{0:T(1024)}, f32[16384]{0:T(1024)}), (f32[16384]{0:T(1024)}, f32[16384]{0:T(1024)})) %all-reduce.10.cloned.1.call-update) | async-done | bytes 131088 | tf_op jit(solution)/shard_map/psum | solution.py:46
  1104.0 0.9 broadcast_divide_fusion
  1104.9 16.1 %fusion.35 = f32[1,256]{1,0:T(1,128)S(1)} fusion(f32[256,16384]{1,0:T(8,128)} %copy-done.1, f32[16384,1]{0,1:T(1,128)S(1)} %bitcast.57), kind=kOutput, calls=%fused_computation.65 | convolution fusion | flops 50331648 | bytes 16843776 | tf_op jit(solution)/shard_map/dot_general | solution.py:30
  1121.0 1.2 convolution_bitcast_fusion
  1122.3 14.9 %all-reduce.3 = (f32[4]{0:T(128)S(1)}, f32[256]{0:T(256)S(1)}) all-reduce(f32[4]{0:T(128)S(1)} %convolution_bitcast_fusion, f32[256]{0:T(256)S(1)} %bitcast.73), channel_id=1, replica_groups=mesh['dp'=32,'proto'=8] {'proto'}, use_global_device_ids=true, to_apply=%region_7.8 | all-reduce | flops 260 | bytes 2080 | tf_op jit(solution)/shard_map/psum | solution.py:52
  1137.2 9.4 multiply_convert_fusion
  1146.6 0.8 multiply_convert_fusion.2
  (35 shorter events, 3.6 us)
Async XLA Ops:
  7.2 3.1 copy-start
  7.2 137.5 %all-gather.5.cloned.1.call-start = ((), (), s32[]{:S(2)}) async-start(), calls=%async_computation.1 | async-start | bytes 12976128 | tf_op jit(solution)/shard_map/all_gather | solution.py:41
  7.9 265.5 %all-gather.3.cloned.1.call-start = ((), (), s32[]{:S(2)}) async-start(), calls=%async_computation | async-start | bytes 12976128 | tf_op jit(solution)/shard_map/all_gather | solution.py:42
  8.7 518.9 %all-reduce.14.cloned.1.call-start = ((), (), s32[]{:S(2)}) async-start(), calls=%async_computation.4 | async-start | bytes 262144 | tf_op jit(solution)/shard_map/psum | solution.py:46
  160.6 5.7 copy-start.1
  166.3 114.4 %copy-start.4 = (bf16[4,384]{1,0:T(4,128)(2,1)S(1)}, bf16[4,384]{1,0:T(4,128)(2,1)}, u32[]{:S(2)}) copy-start(bf16[4,384]{1,0:T(4,128)(2,1)} %param.5) | copy-start | bytes 9220
  288.5 527.2 %all-reduce.12.cloned.1.call-start = ((), (), s32[]{:S(2)}) async-start(), calls=%async_computation.3 | async-start | bytes 262144 | tf_op jit(solution)/shard_map/psum | solution.py:46
  574.0 530.1 %all-reduce.10.cloned.1.call-start = ((), (), s32[]{:S(2)}) async-start(), calls=%async_computation.2 | async-start | bytes 262144 | tf_op jit(solution)/shard_map/psum | solution.py:46
  815.7 17.2 %copy-start.2 = (f32[16384]{0:T(1024)S(1)}, f32[16384]{0:T(1024)}, u32[]{:S(2)}) copy-start(f32[16384]{0:T(1024)} %get-tuple-element.4) | copy-start | bytes 196612
  1104.0 17.0 %copy-start.3 = (f32[16384]{0:T(1024)S(1)}, f32[16384]{0:T(1024)}, u32[]{:S(2)}) copy-start(f32[16384]{0:T(1024)} %get-tuple-element.2) | copy-start | bytes 196612
Sparse Core Ops, SparseCore 0:
  10.6 134.0 all-gather.4
  147.3 126.1 all-gather.2
  288.6 238.9 all-reduce.13
  574.1 241.5 all-reduce.11
  862.4 241.5 all-reduce.9
where the time goes:
time: 1160 us; the launch traced here: 1150 us
  waiting for transfers between devices  954 us (82%)
  matrix products  104 us (9%)
  blocking collectives  44.7 us (4%)
  other arithmetic  29.9 us (3%)
  between operations  14.1 us (1%)
    psum x3, waiting for transfers between devices, per_device(): lax.psum((column_terms(patch_row_scale, patch_kernel), column_terms(cls_r...  722 us
    all_gather x1, waiting for transfers between devices, per_device(): lax.all_gather(patch_protos, 'dp', axis=1, tiled=True)  131 us
    all_gather x1, waiting for transfers between devices, per_device(): lax.all_gather(cls_protos, 'dp', axis=1, tiled=True)  98.5 us
    dot_general x6, matrix products, row_terms(): return jnp.dot(kernel, col_scale, precision=lax.Precision.HIGHEST)  52.1 us
    psum x3, blocking collectives, per_device(): lax.psum((row_terms(patch_kernel, patch_col_scale), row_terms(cls_kernel,...  44.7 us
    dot_general x6, matrix products, column_terms(): return jnp.dot(row_scale, kernel, precision=lax.Precision.HIGHEST)  36.3 us
  transfers between devices with their start and end apart: 5, of which 5 were waited for; matrix products, arithmetic and copies ran while one was open for 3% of the time, Pallas kernels for 0%

commit v1 on v0

v1 whole, which is shorter than its diff:
```python
import functools

import jax
import jax.numpy as jnp
import numpy as np
from jax import lax
from jax.experimental import pallas as pl
from jax.experimental.pallas import tpu as pltpu
from jax.sharding import PartitionSpec as P

PROTOS = 131072
ITERS = 3
TEMP = 0.07
SLOPE = float(1.0 / (TEMP * np.log(2.0)))
F32 = jnp.float32
BF16 = jnp.bfloat16
BOTH = ("dp", "proto")
MIB = 1 << 20

NZ, NX = 8, 4


def coords(g):
    d, p = g // 8, g % 8
    return d % 2, (d // 2) % NZ, d // (2 * NZ), p % NX, p // NX


def flat(core, z, yh, x, yl):
    return ((yh * NZ + z) * 2 + core) * 8 + yl * NX + x


def swap(dcore=0, dyh=0, dyl=0):
    pairs = []
    for g in range(256):
        core, z, yh, x, yl = coords(g)
        pairs.append((g, flat(core ^ dcore, z, yh ^ dyh, x, yl ^ dyl)))
    return pairs


def groups(key):
    found = {}
    for g in range(256):
        found.setdefault(key(*coords(g)), []).append(g)
    return [found[k] for k in sorted(found)]


CORE = swap(dcore=1)
Y_STEPS = ((1, 1), (1, 0), (0, 1))
GROUPS_Z = groups(lambda core, z, yh, x, yl: (core, yh, x, yl))
GROUPS_ZX = groups(lambda core, z, yh, x, yl: (core, yh, yl))


def exchange(value, group):
    return lax.all_to_all(value, BOTH, 0, 0, axis_index_groups=group, tiled=True)


VM = pl.BlockSpec(memory_space=pltpu.VMEM)
SM = pl.BlockSpec(memory_space=pltpu.SMEM)


def call(body, out_shape, n_in, name, scratch=(), smem_first=False, limit=24):
    specs = [VM] * n_in
    if smem_first:
        specs[0] = SM
    return pl.pallas_call(
        body,
        out_shape=out_shape,
        in_specs=specs,
        out_specs=jax.tree.map(lambda _: VM, out_shape),
        scratch_shapes=list(scratch),
        compiler_params=pltpu.CompilerParams(vmem_limit_bytes=limit * MIB),
        name=name,
    )


def shape(dims, dtype=F32):
    return jax.ShapeDtypeStruct(dims, dtype)


def down(row):
    return jnp.transpose(jnp.broadcast_to(row, (128, 128)))


def across(block):
    return jnp.sum(jnp.transpose(block), axis=0, keepdims=True)


def swapped(rows, step):
    return jnp.concatenate([rows[k ^ step : (k ^ step) + 1] for k in range(8)], axis=0)


def inv_norms(protos):
    wide = protos.astype(F32)
    return SLOPE * lax.rsqrt(jnp.sum(wide * wide, axis=0, keepdims=True) + 1e-06)


def unit(values):
    return (values * lax.rsqrt(jnp.sum(values * values, -1, keepdims=True) + 1e-06)).astype(BF16)


def units_body(where_ref, feat_ref, mask_ref, cls_ref, unit_ref, send_ref):
    for image in range(4):
        pick = lax.broadcasted_iota(jnp.int32, (256, 64), 0) == mask_ref[image : image + 1, :]
        chosen = lax.dot_general(
            pick.astype(BF16), feat_ref[image], (((0,), (0,)), ((), ())), preferred_element_type=F32
        )
        unit_ref[image * 64 : image * 64 + 64, :] = unit(chosen)
    half = unit_ref[pl.ds(pl.multiple_of(where_ref[4] * 128, 128), 128), :]
    cls = unit(cls_ref[...].astype(F32))
    tail = jnp.concatenate([cls.astype(F32), jnp.zeros((12, 384), F32)], axis=0).astype(BF16)
    for z in range(NZ):
        send_ref[z, :128, :] = half
        send_ref[z, 128:, :] = tail


def kernel_body(units_ref, *refs):
    pieces, (kern_ref, sums_ref) = refs[:8], refs[8:]
    for k in range(8):
        protos = pieces[k][...]
        scale = inv_norms(protos)

        def block(z, total):
            rows = pl.ds(pl.multiple_of(z * 128, 128), 128)
            dots = jnp.dot(units_ref[z, :128, :], protos, preferred_element_type=F32)
            value = jnp.exp2(dots * scale - SLOPE)
            kern_ref[rows, k * 512 : k * 512 + 512] = value
            return total + jnp.sum(value.reshape(16, 8, 512), axis=0)

        total = lax.fori_loop(0, NZ, block, jnp.zeros((8, 512), F32), unroll=2)
        sums_ref[k : k + 1, :] = jnp.sum(total, axis=0, keepdims=True)


def cls_step(cls_kern, row_scale):
    wide = down(row_scale)
    cols = [
        1.0 / jnp.sum(cls_kern[:, q * 128 : q * 128 + 128] * wide, axis=0, keepdims=True)
        for q in range(4)
    ]
    total = cls_kern[:, :128] * cols[0]
    for q in range(1, 4):
        total = total + cls_kern[:, q * 128 : q * 128 + 128] * cols[q]
    return cols, across(total)


def cls_body(units_ref, protos_ref, sums_ref, kern_ref, message_ref):
    protos = protos_ref[...]
    dots = jnp.dot(units_ref[...], protos, preferred_element_type=F32)
    kern_ref[...] = jnp.exp2(dots * inv_norms(protos) - SLOPE)
    _, sums = cls_step(kern_ref[...], jnp.ones((1, 128), F32))
    message_ref[:, :512] = sums_ref[...]
    message_ref[:, 512:] = jnp.broadcast_to(sums, (8, 128))


def columns_body(last, got_ref, kern_ref, cls_kern_ref, message_ref, *more):
    total = got_ref[0]
    for k in range(1, 32):
        total = total + got_ref[k]
    row_scale = 1.0 / total[:9]
    cls_kern = cls_kern_ref[...]
    cols, sums = cls_step(cls_kern, row_scale[8:9])
    if last:
        for q in range(4):
            more[0][:, q * 128 : q * 128 + 128] = cls_kern[:, q * 128 : q * 128 + 128] * cols[q]
    acc = more[-1]
    for z in range(NZ):
        wide = down(row_scale[z : z + 1]).reshape(16, 8, 128)
        for t in range(32):
            block = kern_ref[z * 128 : z * 128 + 128, t * 128 : t * 128 + 128]
            part = jnp.sum(block.reshape(16, 8, 128) * wide, axis=0)
            if z == 0:
                acc[:, t * 128 : t * 128 + 128] = part
            else:
                acc[:, t * 128 : t * 128 + 128] += part
    for k in range(8):
        message_ref[k : k + 1, :512] = jnp.sum(acc[:, k * 512 : k * 512 + 512], axis=0, keepdims=True)
    message_ref[:, 512:] = jnp.broadcast_to(sums, (8, 128))


def add_body(mine_ref, other_ref, out_ref):
    out_ref[...] = mine_ref[...] + swapped(other_ref[...], 4)


def rows_body(last, mine_ref, a_ref, b_ref, c_ref, kern_ref, send_ref, wide_ref):
    total = mine_ref[...]
    for ref, (dyh, dyl) in zip((a_ref, b_ref, c_ref), Y_STEPS):
        total = total + swapped(ref[...], dyh * 2 + dyl)
    cols = 1.0 / total[:, :512]
    cls = total[:1, 512:]
    for k in range(8):
        wide_ref[:, k * 512 : k * 512 + 512] = jnp.broadcast_to(cols[k : k + 1], (8, 512))
    sums = []
    for z in range(NZ):
        acc = jnp.zeros((16, 8, 128), F32)
        for t in range(32):
            block = kern_ref[z * 128 : z * 128 + 128, t * 128 : t * 128 + 128]
            acc = acc + block.reshape(16, 8, 128) * wide_ref[:, t * 128 : t * 128 + 128][None]
        sums.append(across(acc.reshape(128, 128)))
    if last:
        own = [cols[k : k + 1, q * 128 : q * 128 + 128] for k in (0, 2, 4, 6) for q in range(4)]
        own = jnp.concatenate(own, axis=0)
        rest = jnp.zeros((6, 128), F32)
        for z in range(NZ):
            block = jnp.concatenate([own, sums[z], cls, rest], axis=0)
            for x in range(NX):
                send_ref[z * NX + x] = block
    else:
        block = jnp.concatenate(sums + [cls, jnp.zeros((7, 128), F32)], axis=0)
        for k in range(32):
            send_ref[k] = block


def settle_body(where_ref, got_ref, cols_ref, sums_ref):
    core, yh, x = where_ref[0], where_ref[2], where_ref[3]
    for z in range(NZ):
        for cr in range(2):
            for yr in range(2):
                row = (jnp.bitwise_xor(yh, yr) * NZ + z) * 2 + jnp.bitwise_xor(core, cr)
                for q in range(4):
                    at = (cr * 2 + yr) * 4 + q
                    cols_ref[row, :, q * 128 : q * 128 + 128] = got_ref[z * NX + x, at : at + 1, :]
    total = got_ref[0, 16:24, :]
    for k in range(1, 32):
        total = total + got_ref[k, 16:24, :]
    sums_ref[...] = total


def final_body(where_ref, protos_ref, units_ref, cols_ref, mine_ref, other_ref, out_ref, wide_ref):
    step = pl.program_id(0)

    @pl.when(step == 0)
    def _():
        yl = where_ref[4]
        mine, other = mine_ref[:1], other_ref[:1]
        first = jnp.where(yl == 0, mine, other)
        second = jnp.where(yl == 0, other, mine)
        wide_ref[:128] = PROTOS / down(first)
        wide_ref[128:] = PROTOS / down(second)

    for piece in range(4):
        protos = protos_ref[:, piece * 512 : piece * 512 + 512]
        scale = inv_norms(protos)
        cols = cols_ref[step * 4 + piece]
        dots = jnp.dot(units_ref[...], protos, preferred_element_type=F32)
        value = jnp.exp2(dots * scale - SLOPE) * cols
        for q in range(4):
            out_ref[:, piece * 512 + q * 128 : piece * 512 + q * 128 + 128] = (
                value[:, q * 128 : q * 128 + 128] * wide_ref[...]
            ).astype(BF16)


def final(where, protos, units, cols, mine, other):
    width = 2048
    return pl.pallas_call(
        final_body,
        out_shape=shape((256, 16384), BF16),
        grid=(16384 // width,),
        in_specs=[
            SM,
            pl.BlockSpec((384, width), lambda i: (0, i)),
            VM,
            VM,
            VM,
            VM,
        ],
        out_specs=pl.BlockSpec((256, width), lambda i: (0, i)),
        scratch_shapes=[pltpu.VMEM((256, 128), F32)],
        compiler_params=pltpu.CompilerParams(vmem_limit_bytes=56 * MIB),
        name="final_scale",
    )(where, protos, units, cols, mine, other)


def per_device(cls_features, patch_features, mask_index, cls_protos, patch_protos):
    dp, proto = lax.axis_index("dp"), lax.axis_index("proto")
    core, z, yh = dp % 2, (dp // 2) % NZ, dp // (2 * NZ)
    x, yl = proto % NX, proto // NX
    where = jnp.stack([core, z, yh, x, yl]).astype(jnp.int32)

    gathered = lax.all_gather(patch_protos, "dp", axis=1, tiled=True)

    near = {(0, 0): patch_protos}
    for dyh, dyl in Y_STEPS:
        near[dyh, dyl] = lax.ppermute(patch_protos, BOTH, swap(dyh=dyh, dyl=dyl))
    pieces = [near[k // 2, k % 2] for k in range(4)]
    pieces += [lax.ppermute(piece, BOTH, CORE) for piece in pieces]

    units, send = call(
        units_body, (shape((256, 384), BF16), shape((NZ, 144, 384), BF16)), 4, "units", smem_first=True
    )(where, patch_features, mask_index, cls_features)
    rows = exchange(send, GROUPS_Z)

    kern, col_sums = call(
        kernel_body, (pltpu.VMEM((1024, 4096), F32), shape((8, 512))), 9, "patch_kernel"
    )(rows, *pieces)

    cls_units = rows[:, 128:132, :]
    other = lax.ppermute(cls_units, BOTH, CORE)
    cls_units = jnp.stack([jnp.where(core == 0, cls_units, other), jnp.where(core == 0, other, cls_units)], 1)
    other = lax.ppermute(cls_units, BOTH, swap(dyh=1))
    cls_units = jnp.stack([jnp.where(yh == 0, cls_units, other), jnp.where(yh == 0, other, cls_units)], 0)
    cls_kern, message = call(cls_body, (shape((128, 512)), shape((8, 640))), 3, "cls_kernel")(
        cls_units.reshape(128, 384), cls_protos, col_sums
    )

    for step in range(ITERS):
        last = step == ITERS - 1
        if step:
            outs = [shape((8, 640))]
            if last:
                outs.append(shape((128, 512)))
            done = call(
                functools.partial(columns_body, last), tuple(outs), 3, "column_sums", [pltpu.VMEM((8, 4096), F32)]
            )(got, kern, cls_kern)
            message = done[0]
        message = call(add_body, shape((8, 640)), 2, "add_core")(message, lax.ppermute(message, BOTH, CORE))
        parts = [lax.ppermute(message, BOTH, swap(dyh=dyh, dyl=dyl)) for dyh, dyl in Y_STEPS]
        send = call(
            functools.partial(rows_body, last),
            shape((32, 24 if last else 16, 128)),
            5,
            "row_sums",
            [pltpu.VMEM((8, 4096), F32)],
        )(message, *parts, kern)
        got = exchange(send, GROUPS_ZX)

    cols, sums = call(settle_body, (shape((32, 1, 512)), shape((8, 128))), 2, "settle", smem_first=True)(where, got)
    other = lax.ppermute(sums, BOTH, swap(dyl=1))
    patch_targets = final(where, gathered, units, cols, sums, other)

    cls_scaled = lax.all_to_all(done[1].reshape(32, 4, 512), "dp", 0, 0, tiled=True)
    cls_rows = PROTOS / lax.dynamic_slice(sums[1], (dp * 4,), (4,))
    cls_targets = (cls_scaled.transpose(1, 0, 2) * cls_rows[:, None, None]).astype(BF16).reshape(4, 16384)
    return (cls_targets, patch_targets)


def solution(mesh):
    return jax.shard_map(
        per_device,
        mesh=mesh,
        in_specs=(
            P("dp", None),
            P("dp", None, None),
            P("dp", None),
            P(None, ("proto", "dp")),
            P(None, ("proto", "dp")),
        ),
        out_specs=(P("dp", "proto"), P("dp", "proto")),
        check_vma=False,
    )
```

time: 1160 us -> 214 us (0.18)
  waiting for transfers between devices: 954 us -> 58.7 us
  matrix products: 104 us -> 0 us
  starting transfers between devices: 0.2 us -> 49.3 us
  Pallas kernels: 0 us -> 35.1 us
  other arithmetic: 29.9 us -> 1.04 us
    psum x3 -> x0, waiting for transfers between devices: 722 us -> none  [per_device(): lax.psum((column_terms(patch_row_scale, patch_kernel), column_terms(cls_r...]
    all_gather x2 -> x1, waiting for transfers between devices: 230 us -> 0.01 us  [per_device(): gathered = lax.all_gather(patch_protos, 'dp', axis=1, tiled=True)]
    dot_general x14 -> x0, matrix products: 104 us -> none  [the longest x6 52.1 us: row_terms(): return jnp.dot(kernel, col_scale, precision=lax.Precision.HIGHEST)]
    all_to_all x0 -> x3, waiting for transfers between devices: none -> 47.3 us  [the longest x2 35.2 us: exchange(): lax.all_to_all(value, BOTH, 0, 0, axis_index_groups=group, tiled=True)]
    psum x3 -> x0, blocking collectives: 44.7 us -> none  [per_device(): lax.psum((row_terms(patch_kernel, patch_col_scale), row_terms(cls_kernel,...]
    all_to_all x0 -> x2, blocking collectives: none -> 35.1 us  [exchange(): lax.all_to_all(value, BOTH, 0, 0, axis_index_groups=group, tiled=True)]
    pallas_call x0 -> x13, Pallas kernels: none -> 35.1 us  [the longest x1 12.6 us: final(): pl.pallas_call(final_body, out_shape=shape((256, 16384), BF16), grid=(163...]
    ppermute x0 -> x22, starting transfers between devices: none -> 28 us  [the longest x9 9.76 us: per_device(): lax.ppermute(message, BOTH, swap(dyh=dyh, dyl=dyl))]
  transfers between devices with their start and end apart: 5 -> 26, of which waited for: 5 -> 12; matrix products, arithmetic and copies ran while one was open for 3% -> 1% of each run, Pallas kernels for 0% -> 11%
where the time goes in v1:
time: 214 us; the launch traced here: 213 us
  waiting for transfers between devices  58.7 us (27%)
  starting transfers between devices  49.3 us (23%)
  Pallas kernels  35.1 us (16%)
  blocking collectives  35.1 us (16%)
  local copies, waits for them, and re-layouts  19.3 us (9%)
  between operations  14.3 us (7%)
    all_to_all x2, waiting for transfers between devices, exchange(): lax.all_to_all(value, BOTH, 0, 0, axis_index_groups=group, tiled=True)  35.2 us
    all_to_all x2, blocking collectives, exchange(): lax.all_to_all(value, BOTH, 0, 0, axis_index_groups=group, tiled=True)  35.1 us
    unnamed x32, local copies, waits for them, and re-layouts  18.4 us
    all_to_all x2, starting transfers between devices, exchange(): lax.all_to_all(value, BOTH, 0, 0, axis_index_groups=group, tiled=True)  12.9 us
    pallas_call x1, Pallas kernels, final(): pl.pallas_call(final_body, out_shape=shape((256, 16384), BF16), grid=(163...  12.6 us
    all_to_all x1, waiting for transfers between devices, per_device(): lax.all_to_all(done[1].reshape(32, 4, 512), 'dp', 0, 0, tiled=True)  12.1 us
    pallas_call x1, Pallas kernels, per_device(): call(kernel_body, (pltpu.VMEM((1024, 4096), F32), shape((8, 512))), 9, 'p...  11.8 us
    ppermute x9, starting transfers between devices, per_device(): lax.ppermute(message, BOTH, swap(dyh=dyh, dyl=dyl))  9.76 us
  transfers between devices with their start and end apart: 26, of which 12 were waited for; matrix products, arithmetic and copies ran while one was open for 1% of the time, Pallas kernels for 11%

profile of v1, /device:TPU:1, one launch (start us, length us, event | category | flops | bytes accessed | tf_op | source)
XLA Modules:
  0.0 212.8 jit_solution(12950759896862145436)
XLA Ops:
  8.0 1.1 copy-done.3
  10.5 1.9 units.1
  13.1 9.0 %all-to-all-start = ((bf16[8,144,384]{2,1,0:T(8,128)(2,1)}), bf16[8,144,384]{2,1,0:T(8,128)(2,1)S(1)}, u32[]{:S(2)}, u32[]{:S(2)}) async-start(bf16[8,144,384]{2,1,0:T(8,128)(2,1)} %get-tuple-element.12), calls=%async_computation | async-start | bytes 1769472 | tf_op jit(solution)/shard_map/all_to_all | solution.py:54
  22.1 1.3 collective-permute-start.2
  23.4 2.6 %collective-permute-start.3 = (bf16[384,512]{1,0:T(8,128)(2,1)}, bf16[384,512]{1,0:T(8,128)(2,1)S(1)}, u32[]{:S(2)}, u32[]{:S(2)}) collective-permute-start(bf16[384,512]{1,0:T(8,128)(2,1)} %refs_0_.1), channel_id=1, source_target_pairs={{0,128},{1,129},{2,130},{3,131},{4,132},{5,133},{6,134},{7,135},{8... | collective-permute-start | bytes 1179656 | tf_op jit(solution)/shard_map/ppermute | solution.py:282
  26.1 23.3 %all-to-all-done.units_ref = bf16[8,144,384]{2,1,0:T(8,128)(2,1)S(1)} async-done(((bf16[8,144,384]{2,1,0:T(8,128)(2,1)}), bf16[8,144,384]{2,1,0:T(8,128)(2,1)S(1)}, u32[]{:S(2)}, u32[]{:S(2)}) %all-to-all-start) | async-done | bytes 884768 | tf_op jit(solution)/shard_map/all_to_all | solution.py:54
  49.3 1.0 collective-permute-start
  51.7 5.1 %collective-permute-start.1 = (bf16[8,2,4,384]{3,2,0,1:T(4,128)(2,1)S(1)}, bf16[8,2,4,384]{3,2,0,1:T(4,128)(2,1)S(1)}, u32[]{:S(2)}, u32[]{:S(2)}) collective-permute-start(bf16[8,2,4,384]{3,2,0,1:T(4,128)(2,1)S(1)} %pad_maximum_fusion.1), channel_id=1, source_target_pairs={{0,128},{1,129},{2,130},{3,131},{4,132},{5,133},{6,134},{7,135},{8... | collective-permute-start | bytes 147464 | tf_op jit(solution)/shard_map/ppermute | solution.py:298
  57.9 11.8 %patch_kernel.1 = (f32[1024,4096]{1,0:T(8,128)S(1)}, f32[8,512]{1,0:T(8,128)S(1)}) custom-call(bf16[8,144,384]{2,1,0:T(8,128)(2,1)S(1)} %all-to-all-done.units_ref, bf16[384,512]{1,0:T(8,128)(2,1)S(1)} %copy-done.2, bf16[384,512]{1,0:T(8,128)(2,1)S(1)} %collective-permute-done.2.refs_1_, bf16[384,512]{1,0:T(8,128)(2,1)S(1)} %collective-permute-done.3.refs_2_, ...), custom_call_target="tpu_custom_call" | custom-call | tf_op jit(solution)/shard_map/patch_kernel/pallas_call | solution.py:291
  69.7 5.8 %copy-done = f32[1024,4096]{1,0:T(8,128)} copy-done((f32[1024,4096]{1,0:T(8,128)}, f32[1024,4096]{1,0:T(8,128)S(1)}, u32[]{:S(2)}) %copy-start) | copy-done | bytes 16777240
  78.5 1.9 collective-permute-start.10
  82.3 2.3 %collective-permute-done.11.b_ref = f32[8,640]{1,0:T(8,128)S(1)} collective-permute-done((f32[8,640]{1,0:T(8,128)S(1)}, f32[8,640]{1,0:T(8,128)S(1)}, u32[]{:S(2)}, u32[]{:S(2)}) %collective-permute-start.11) | collective-permute-done | bytes 20512 | tf_op jit(solution)/shard_map/ppermute | solution.py:315
  84.6 6.2 %copy-done.1 = f32[1024,4096]{1,0:T(8,128)S(1)} copy-done((f32[1024,4096]{1,0:T(8,128)S(1)}, f32[1024,4096]{1,0:T(8,128)}, u32[]{:S(2)}) %copy-start.1) | copy-done | bytes 16777240
  90.8 1.2 row_sums.3
  92.1 15.8 %all_to_all.25.got_ref = f32[32,16,128]{2,1,0:T(8,128)S(1)} all-to-all(f32[32,16,128]{2,1,0:T(8,128)S(1)} %row_sums.3), channel_id=1, replica_groups={{0,1,2,3,16,17,18,19,32,33,34,35,48,49,50,51,64,65,66,67,80,81,82,83,96..., dimensions={0} | all-to-all | bytes 524288 | tf_op jit(solution)/shard_map/all_to_all | solution.py:54
  107.8 1.4 column_sums.2.mine_ref
  109.2 3.8 %collective-permute-start.13 = (f32[8,640]{1,0:T(8,128)S(1)}, f32[8,640]{1,0:T(8,128)S(1)}, u32[]{:S(2)}, u32[]{:S(2)}) collective-permute-start(f32[8,640]{1,0:T(8,128)S(1)} %column_sums.2.mine_ref), channel_id=1, source_target_pairs={{0,8},{1,9},{2,10},{3,11},{4,12},{5,13},{6,14},{7,15},{8,0},{9,1},... | collective-permute-start | bytes 61448 | tf_op jit(solution)/shard_map/ppermute | solution.py:314
  113.9 1.8 collective-permute-start.14
  117.2 2.4 %collective-permute-done.14.a_ref = f32[8,640]{1,0:T(8,128)S(1)} collective-permute-done((f32[8,640]{1,0:T(8,128)S(1)}, f32[8,640]{1,0:T(8,128)S(1)}, u32[]{:S(2)}, u32[]{:S(2)}) %collective-permute-start.14) | collective-permute-done | bytes 20512 | tf_op jit(solution)/shard_map/ppermute | solution.py:315
  119.9 1.3 row_sums.4
  121.3 19.4 %all_to_all.26.got_ref = f32[32,16,128]{2,1,0:T(8,128)S(1)} all-to-all(f32[32,16,128]{2,1,0:T(8,128)S(1)} %row_sums.4), channel_id=1, replica_groups={{0,1,2,3,16,17,18,19,32,33,34,35,48,49,50,51,64,65,66,67,80,81,82,83,96..., dimensions={0} | all-to-all | bytes 524288 | tf_op jit(solution)/shard_map/all_to_all | solution.py:54
  140.6 1.6 column_sums.3
  142.2 2.5 %collective-permute-start.17 = (f32[8,640]{1,0:T(8,128)S(1)}, f32[8,640]{1,0:T(8,128)S(1)}, u32[]{:S(2)}, u32[]{:S(2)}) collective-permute-start(f32[8,640]{1,0:T(8,128)S(1)} %get-tuple-element.18.mine_ref), channel_id=1, source_target_pairs={{0,8},{1,9},{2,10},{3,11},{4,12},{5,13},{6,14},{7,15},{8,0},{9,1},... | collective-permute-start | bytes 61448 | tf_op jit(solution)/shard_map/ppermute | solution.py:314
  145.6 1.7 collective-permute-start.18
  147.8 1.1 collective-permute-start.20
  149.5 2.0 collective-permute-done.19.b_ref
  151.5 2.2 %row_sums.5 = f32[32,24,128]{2,1,0:T(8,128)} custom-call(f32[8,640]{1,0:T(8,128)S(1)} %add_core.5.mine_ref, f32[8,640]{1,0:T(8,128)S(1)} %collective-permute-done.18.a_ref, f32[8,640]{1,0:T(8,128)S(1)} %collective-permute-done.19.b_ref, f32[8,640]{1,0:T(8,128)S(1)} %collective-permute-done.20.c_ref, f32[1024,4096]{1,0:T(8,128)S(1)} %bitcast.19), custom_call_target="tpu_custom_call" | custom-call | tf_op jit(solution)/shard_map/row_sums/pallas_call | solution.py:316
  153.7 3.9 %all-to-all-start.4 = ((f32[32,24,128]{2,1,0:T(8,128)}), f32[32,24,128]{2,1,0:T(8,128)S(1)}, u32[]{:S(2)}, u32[]{:S(2)}) async-start(f32[32,24,128]{2,1,0:T(8,128)} %row_sums.5), calls=%async_computation.4 | async-start | bytes 786432 | tf_op jit(solution)/shard_map/all_to_all | solution.py:54
  158.4 11.9 %all-to-all-done.4.got_ref = f32[32,24,128]{2,1,0:T(8,128)S(1)} async-done(((f32[32,24,128]{2,1,0:T(8,128)}), f32[32,24,128]{2,1,0:T(8,128)S(1)}, u32[]{:S(2)}, u32[]{:S(2)}) %all-to-all-start.4) | async-done | bytes 393248 | tf_op jit(solution)/shard_map/all_to_all | solution.py:54
  170.3 8.3 %all-to-all-start.3 = ((f32[32,4,512]{2,1,0:T(4,128)}), f32[32,4,512]{2,1,0:T(4,128)S(1)}, u32[]{:S(2)}, u32[]{:S(2)}) async-start(f32[32,4,512]{2,1,0:T(4,128)} %reshape.22), calls=%async_computation.3 | async-start | bytes 524288 | tf_op jit(solution)/shard_map/all_to_all | solution.py:329
  179.9 12.1 %all-to-all-done.3 = f32[32,4,512]{2,1,0:T(4,128)S(1)} async-done(((f32[32,4,512]{2,1,0:T(4,128)}), f32[32,4,512]{2,1,0:T(4,128)S(1)}, u32[]{:S(2)}, u32[]{:S(2)}) %all-to-all-start.3) | async-done | bytes 262176 | tf_op jit(solution)/shard_map/all_to_all | solution.py:329
  193.4 12.6 %final_scale.1 = bf16[256,16384]{1,0:T(8,128)(2,1)} custom-call(s32[5]{0:T(128)} %copy-done.7, bf16[384,16384]{1,0:T(8,128)(2,1)} %all-gather.2.cloned.1.call-done.protos_ref, bf16[256,384]{1,0:T(8,128)(2,1)} %copy-done.5, f32[32,1,512]{2,1,0:T(1,128)} %copy-done.6, f32[8,128]{1,0:T(8,128)} %copy-done.8, f32[8,128]{1,0:T(8,128)} %copy-done.11), custom_call_target="tpu_custom_call" | custom-call | tf_op jit(solution)/shard_map/final_scale/pallas_call | solution.py:253
  (81 shorter events, 17.9 us)
Async XLA Ops:
  7.2 185.6 %all-gather.2.cloned.1.call-start = ((), (), s32[]{:S(2)}) async-start(), calls=%async_computation.5 | async-start | bytes 12976128 | tf_op jit(solution)/shard_map/all_gather | solution.py:278
  10.5 168.1 %copy-start.7 = (s32[5]{0:T(128)}, s32[5]{0:T(128)S(1)}, u32[]{:S(2)}) copy-start(s32[5]{0:T(128)S(1)} %stack.41.where_ref) | copy-start | bytes 64
  13.1 36.2 %all-to-all-start = ((bf16[8,144,384]{2,1,0:T(8,128)(2,1)}), bf16[8,144,384]{2,1,0:T(8,128)(2,1)S(1)}, u32[]{:S(2)}, u32[]{:S(2)}) async-start(bf16[8,144,384]{2,1,0:T(8,128)(2,1)} %get-tuple-element.12), calls=%async_computation | async-start | bytes 1769472 | tf_op jit(solution)/shard_map/all_to_all | solution.py:54
  22.1 28.3 %collective-permute-start.2 = (bf16[384,512]{1,0:T(8,128)(2,1)}, bf16[384,512]{1,0:T(8,128)(2,1)S(1)}, u32[]{:S(2)}, u32[]{:S(2)}) collective-permute-start(bf16[384,512]{1,0:T(8,128)(2,1)} %refs_0_.1), channel_id=1, source_target_pairs={{0,4},{1,5},{2,6},{3,7},{4,0},{5,1},{6,2},{7,3},{8,12},{9,13},{10,... | collective-permute-start | bytes 1179656 | tf_op jit(solution)/shard_map/ppermute | solution.py:282
  23.4 27.4 %collective-permute-start.3 = (bf16[384,512]{1,0:T(8,128)(2,1)}, bf16[384,512]{1,0:T(8,128)(2,1)S(1)}, u32[]{:S(2)}, u32[]{:S(2)}) collective-permute-start(bf16[384,512]{1,0:T(8,128)(2,1)} %refs_0_.1), channel_id=1, source_target_pairs={{0,128},{1,129},{2,130},{3,131},{4,132},{5,133},{6,134},{7,135},{8... | collective-permute-start | bytes 1179656 | tf_op jit(solution)/shard_map/ppermute | solution.py:282
  26.1 24.9 %collective-permute-start.4 = (bf16[384,512]{1,0:T(8,128)(2,1)}, bf16[384,512]{1,0:T(8,128)(2,1)S(1)}, u32[]{:S(2)}, u32[]{:S(2)}) collective-permute-start(bf16[384,512]{1,0:T(8,128)(2,1)} %refs_0_.1), channel_id=1, source_target_pairs={{0,132},{1,133},{2,134},{3,135},{4,128},{5,129},{6,130},{7,131},{8... | collective-permute-start | bytes 1179656 | tf_op jit(solution)/shard_map/ppermute | solution.py:282
  49.3 2.3 %collective-permute-start = (bf16[8,4,384]{2,1,0:T(4,128)(2,1)S(1)}, bf16[8,4,384]{2,1,0:T(4,128)(2,1)S(1)}, u32[]{:S(2)}, u32[]{:S(2)}) collective-permute-start(bf16[8,4,384]{2,1,0:T(4,128)(2,1)S(1)} %slice.8), channel_id=1, source_target_pairs={{0,8},{1,9},{2,10},{3,11},{4,12},{5,13},{6,14},{7,15},{8,0},{9,1},... | collective-permute-start | bytes 73736 | tf_op jit(solution)/shard_map/ppermute | solution.py:296
  50.3 6.5 %collective-permute-start.5 = (bf16[384,512]{1,0:T(8,128)(2,1)}, bf16[384,512]{1,0:T(8,128)(2,1)S(1)}, u32[]{:S(2)}, u32[]{:S(2)}) collective-permute-start(bf16[384,512]{1,0:T(8,128)(2,1)} %refs_0_.1), channel_id=1, source_target_pairs={{0,8},{1,9},{2,10},{3,11},{4,12},{5,13},{6,14},{7,15},{8,0},{9,1},... | collective-permute-start | bytes 1179656 | tf_op jit(solution)/shard_map/ppermute | solution.py:284
  50.5 6.4 %collective-permute-start.6 = (bf16[384,512]{1,0:T(8,128)(2,1)S(1)}, bf16[384,512]{1,0:T(8,128)(2,1)S(1)}, u32[]{:S(2)}, u32[]{:S(2)}) collective-permute-start(bf16[384,512]{1,0:T(8,128)(2,1)S(1)} %collective-permute-done.2.refs_1_), channel_id=1, source_target_pairs={{0,8},{1,9},{2,10},{3,11},{4,12},{5,13},{6,14},{7,15},{8,0},{9,1},... | collective-permute-start | bytes 1179656 | tf_op jit(solution)/shard_map/ppermute | solution.py:284
  50.9 6.0 %collective-permute-start.7 = (bf16[384,512]{1,0:T(8,128)(2,1)S(1)}, bf16[384,512]{1,0:T(8,128)(2,1)S(1)}, u32[]{:S(2)}, u32[]{:S(2)}) collective-permute-start(bf16[384,512]{1,0:T(8,128)(2,1)S(1)} %collective-permute-done.3.refs_2_), channel_id=1, source_target_pairs={{0,8},{1,9},{2,10},{3,11},{4,12},{5,13},{6,14},{7,15},{8,0},{9,1},... | collective-permute-start | bytes 1179656 | tf_op jit(solution)/shard_map/ppermute | solution.py:284
  51.0 5.9 %collective-permute-start.8 = (bf16[384,512]{1,0:T(8,128)(2,1)S(1)}, bf16[384,512]{1,0:T(8,128)(2,1)}, u32[]{:S(2)}, u32[]{:S(2)}) collective-permute-start(bf16[384,512]{1,0:T(8,128)(2,1)S(1)} %collective-permute-done.4.refs_3_), channel_id=1, source_target_pairs={{0,8},{1,9},{2,10},{3,11},{4,12},{5,13},{6,14},{7,15},{8,0},{9,1},... | collective-permute-start | bytes 1179656 | tf_op jit(solution)/shard_map/ppermute | solution.py:284
  51.7 23.8 %collective-permute-start.1 = (bf16[8,2,4,384]{3,2,0,1:T(4,128)(2,1)S(1)}, bf16[8,2,4,384]{3,2,0,1:T(4,128)(2,1)S(1)}, u32[]{:S(2)}, u32[]{:S(2)}) collective-permute-start(bf16[8,2,4,384]{3,2,0,1:T(4,128)(2,1)S(1)} %pad_maximum_fusion.1), channel_id=1, source_target_pairs={{0,128},{1,129},{2,130},{3,131},{4,132},{5,133},{6,134},{7,135},{8... | collective-permute-start | bytes 147464 | tf_op jit(solution)/shard_map/ppermute | solution.py:298
  77.1 1.4 collective-permute-start.9
  78.5 3.8 %collective-permute-start.10 = (f32[8,640]{1,0:T(8,128)S(1)}, f32[8,640]{1,0:T(8,128)S(1)}, u32[]{:S(2)}, u32[]{:S(2)}) collective-permute-start(f32[8,640]{1,0:T(8,128)S(1)} %add_core.3.mine_ref), channel_id=1, source_target_pairs={{0,132},{1,133},{2,134},{3,135},{4,128},{5,129},{6,130},{7,131},{8... | collective-permute-start | bytes 61448 | tf_op jit(solution)/shard_map/ppermute | solution.py:315
  80.4 4.2 %collective-permute-start.11 = (f32[8,640]{1,0:T(8,128)S(1)}, f32[8,640]{1,0:T(8,128)S(1)}, u32[]{:S(2)}, u32[]{:S(2)}) collective-permute-start(f32[8,640]{1,0:T(8,128)S(1)} %add_core.3.mine_ref), channel_id=1, source_target_pairs={{0,128},{1,129},{2,130},{3,131},{4,132},{5,133},{6,134},{7,135},{8... | collective-permute-start | bytes 61448 | tf_op jit(solution)/shard_map/ppermute | solution.py:315
  80.8 3.8 %collective-permute-start.12 = (f32[8,640]{1,0:T(8,128)S(1)}, f32[8,640]{1,0:T(8,128)S(1)}, u32[]{:S(2)}, u32[]{:S(2)}) collective-permute-start(f32[8,640]{1,0:T(8,128)S(1)} %add_core.3.mine_ref), channel_id=1, source_target_pairs={{0,4},{1,5},{2,6},{3,7},{4,0},{5,1},{6,2},{7,3},{8,12},{9,13},{10,... | collective-permute-start | bytes 61448 | tf_op jit(solution)/shard_map/ppermute | solution.py:315
  90.8 29.1 %slice-start = ((s8[16777216]{0:T(1024)(128)(4,1)}), s8[4194304]{0:T(1024)(128)(4,1)S(1)}, s32[]{:S(2)}) async-start(s8[16777216]{0:T(1024)(128)(4,1)} %bitcast.18), calls=%async_computation.6 | async-start | bytes 8388608
  90.8 29.1 %slice-start.1 = ((s8[16777216]{0:T(1024)(128)(4,1)}), s8[4194304]{0:T(1024)(128)(4,1)S(1)}, s32[]{:S(2)}) async-start(s8[16777216]{0:T(1024)(128)(4,1)} %bitcast.18), calls=%async_computation.7 | async-start | bytes 8388608
  92.0 27.9 %slice-start.2 = ((s8[16777216]{0:T(1024)(128)(4,1)}), s8[4194304]{0:T(1024)(128)(4,1)S(1)}, s32[]{:S(2)}) async-start(s8[16777216]{0:T(1024)(128)(4,1)} %bitcast.18), calls=%async_computation.8 | async-start | bytes 8388608
  107.8 12.1 %slice-start.3 = ((s8[16777216]{0:T(1024)(128)(4,1)}), s8[4194304]{0:T(1024)(128)(4,1)S(1)}, s32[]{:S(2)}) async-start(s8[16777216]{0:T(1024)(128)(4,1)} %bitcast.18), calls=%async_computation.9 | async-start | bytes 8388608
  109.2 4.7 %collective-permute-start.13 = (f32[8,640]{1,0:T(8,128)S(1)}, f32[8,640]{1,0:T(8,128)S(1)}, u32[]{:S(2)}, u32[]{:S(2)}) collective-permute-start(f32[8,640]{1,0:T(8,128)S(1)} %column_sums.2.mine_ref), channel_id=1, source_target_pairs={{0,8},{1,9},{2,10},{3,11},{4,12},{5,13},{6,14},{7,15},{8,0},{9,1},... | collective-permute-start | bytes 61448 | tf_op jit(solution)/shard_map/ppermute | solution.py:314
  113.9 5.7 %collective-permute-start.14 = (f32[8,640]{1,0:T(8,128)S(1)}, f32[8,640]{1,0:T(8,128)S(1)}, u32[]{:S(2)}, u32[]{:S(2)}) collective-permute-start(f32[8,640]{1,0:T(8,128)S(1)} %add_core.4.mine_ref), channel_id=1, source_target_pairs={{0,132},{1,133},{2,134},{3,135},{4,128},{5,129},{6,130},{7,131},{8... | collective-permute-start | bytes 61448 | tf_op jit(solution)/shard_map/ppermute | solution.py:315
  115.8 4.1 %collective-permute-start.15 = (f32[8,640]{1,0:T(8,128)S(1)}, f32[8,640]{1,0:T(8,128)S(1)}, u32[]{:S(2)}, u32[]{:S(2)}) collective-permute-start(f32[8,640]{1,0:T(8,128)S(1)} %add_core.4.mine_ref), channel_id=1, source_target_pairs={{0,128},{1,129},{2,130},{3,131},{4,132},{5,133},{6,134},{7,135},{8... | collective-permute-start | bytes 61448 | tf_op jit(solution)/shard_map/ppermute | solution.py:315
  116.6 3.3 %collective-permute-start.16 = (f32[8,640]{1,0:T(8,128)S(1)}, f32[8,640]{1,0:T(8,128)S(1)}, u32[]{:S(2)}, u32[]{:S(2)}) collective-permute-start(f32[8,640]{1,0:T(8,128)S(1)} %add_core.4.mine_ref), channel_id=1, source_target_pairs={{0,4},{1,5},{2,6},{3,7},{4,0},{5,1},{6,2},{7,3},{8,12},{9,13},{10,... | collective-permute-start | bytes 61448 | tf_op jit(solution)/shard_map/ppermute | solution.py:315
  142.2 3.4 %collective-permute-start.17 = (f32[8,640]{1,0:T(8,128)S(1)}, f32[8,640]{1,0:T(8,128)S(1)}, u32[]{:S(2)}, u32[]{:S(2)}) collective-permute-start(f32[8,640]{1,0:T(8,128)S(1)} %get-tuple-element.18.mine_ref), channel_id=1, source_target_pairs={{0,8},{1,9},{2,10},{3,11},{4,12},{5,13},{6,14},{7,15},{8,0},{9,1},... | collective-permute-start | bytes 61448 | tf_op jit(solution)/shard_map/ppermute | solution.py:314
  145.6 3.8 %collective-permute-start.18 = (f32[8,640]{1,0:T(8,128)S(1)}, f32[8,640]{1,0:T(8,128)S(1)}, u32[]{:S(2)}, u32[]{:S(2)}) collective-permute-start(f32[8,640]{1,0:T(8,128)S(1)} %add_core.5.mine_ref), channel_id=1, source_target_pairs={{0,132},{1,133},{2,134},{3,135},{4,128},{5,129},{6,130},{7,131},{8... | collective-permute-start | bytes 61448 | tf_op jit(solution)/shard_map/ppermute | solution.py:315
  147.3 4.1 %collective-permute-start.19 = (f32[8,640]{1,0:T(8,128)S(1)}, f32[8,640]{1,0:T(8,128)S(1)}, u32[]{:S(2)}, u32[]{:S(2)}) collective-permute-start(f32[8,640]{1,0:T(8,128)S(1)} %add_core.5.mine_ref), channel_id=1, source_target_pairs={{0,128},{1,129},{2,130},{3,131},{4,132},{5,133},{6,134},{7,135},{8... | collective-permute-start | bytes 61448 | tf_op jit(solution)/shard_map/ppermute | solution.py:315
  147.8 3.7 %collective-permute-start.20 = (f32[8,640]{1,0:T(8,128)S(1)}, f32[8,640]{1,0:T(8,128)S(1)}, u32[]{:S(2)}, u32[]{:S(2)}) collective-permute-start(f32[8,640]{1,0:T(8,128)S(1)} %add_core.5.mine_ref), channel_id=1, source_target_pairs={{0,4},{1,5},{2,6},{3,7},{4,0},{5,1},{6,2},{7,3},{8,12},{9,13},{10,... | collective-permute-start | bytes 61448 | tf_op jit(solution)/shard_map/ppermute | solution.py:315
  153.7 16.6 %all-to-all-start.4 = ((f32[32,24,128]{2,1,0:T(8,128)}), f32[32,24,128]{2,1,0:T(8,128)S(1)}, u32[]{:S(2)}, u32[]{:S(2)}) async-start(f32[32,24,128]{2,1,0:T(8,128)} %row_sums.5), calls=%async_computation.4 | async-start | bytes 786432 | tf_op jit(solution)/shard_map/all_to_all | solution.py:54
  170.3 21.7 %all-to-all-start.3 = ((f32[32,4,512]{2,1,0:T(4,128)}), f32[32,4,512]{2,1,0:T(4,128)S(1)}, u32[]{:S(2)}, u32[]{:S(2)}) async-start(f32[32,4,512]{2,1,0:T(4,128)} %reshape.22), calls=%async_computation.3 | async-start | bytes 524288 | tf_op jit(solution)/shard_map/all_to_all | solution.py:329
  179.8 13.0 %copy-start.8 = (f32[8,128]{1,0:T(8,128)}, f32[8,128]{1,0:T(8,128)S(1)}, u32[]{:S(2)}) copy-start(f32[8,128]{1,0:T(8,128)S(1)} %get-tuple-element.19.mine_ref) | copy-start | bytes 12292
  179.8 13.0 %collective-permute-start.21 = (f32[8,128]{1,0:T(8,128)S(1)}, f32[8,128]{1,0:T(8,128)S(1)}, u32[]{:S(2)}, u32[]{:S(2)}) collective-permute-start(f32[8,128]{1,0:T(8,128)S(1)} %get-tuple-element.19.mine_ref), channel_id=1, source_target_pairs={{0,4},{1,5},{2,6},{3,7},{4,0},{5,1},{6,2},{7,3},{8,12},{9,13},{10,... | collective-permute-start | bytes 12296 | tf_op jit(solution)/shard_map/ppermute | solution.py:326
  (10 other events, 18.4 us)
Sparse Core Ops, SparseCore 0:
  10.6 153.3 all-gather.1
